TPU v7x, 32 devices: a whole 2x2x4 slice. The times are simulated.
32 devices in a mesh: sy: 4 (over z), sx: 4 (over y, core), tp: 2 (over x).
Axes of the slice: x: 2, y: 2, z: 4, core: 2. Of those that a mesh axis runs over, the one named last changes fastest.
Arguments:
- features: bfloat16 [96, 64, 1408], P('sy', 'sx', 'tp'), may hold values from -6 to 6
- depth_kernel: float32 [7, 7, 1408], P(None, None, 'tp'), may hold values from -0.875 to 0.875
- depth_bias: float32 [1408], P('tp'), may hold values from -1 to 1
- norm_gain: float32 [1408], replicated, may hold values from 0.1 to 1.9
- norm_bias: float32 [1408], replicated, may hold values from -3 to 3
- up_weight: bfloat16 [1408, 5632], P(None, 'tp'), may hold values from -0.15625 to 0.15625
- up_bias: float32 [5632], P('tp'), may hold values from -3 to 3
- response_gain: float32 [5632], P('tp'), may hold values from -4 to 4
- response_shift: float32 [5632], P('tp'), may hold values from -3 to 3
- down_weight: bfloat16 [5632, 1408], P('tp', ('sy', 'sx')), may hold values from -0.078125 to 0.078125
- down_bias: float32 [1408], P('tp'), may hold values from -3 to 3
- tissue: int32 [12, 8], P('sy', 'sx'), may hold values from 0 to 1, as said below
- cotangent: bfloat16 [96, 64, 1408], P('sy', 'sx', 'tp'), may hold values from -6 to 6
Outputs:
- block_out: bfloat16 [96, 64, 1408], P('sy', 'sx', 'tp')
- feature_grad: bfloat16 [96, 64, 1408], P('sy', 'sx', 'tp')
Inputs may be any that keep to these rules, and one draw needn't show every extreme that they name: Each device's block of 3 x 2 tiles holds 1 to 4 tissue tiles; some device's block holds exactly 4.
All inputs are finite; a program needn't handle non-finite values.
Results may differ from a plain program's by a relative error of at most 0.0049.
The roundings to bfloat16 on the way count: a program that leaves them out, or rounds other values in their place, can miss the bound.
Values may be sent and summed in bfloat16 or wider, within the bound.
A program may use at most 128 MiB of HBM per device.

v0:
```python
import jax
import jax.numpy as jnp
from jax import lax
from jax.sharding import PartitionSpec as P

KERNEL = 7
TILE = 8
root_half = 0.7071067811865476
root_two_pi_inv = 0.3989422804014327


def extended(block, sides, width):
    for axis, dim in sides:
        count = lax.axis_size(axis)
        forward = [(i, i + 1) for i in range(count - 1)]
        backward = [(target, source) for source, target in forward]
        low = lax.ppermute(
            lax.slice_in_dim(block, block.shape[dim] - width, None, axis=dim), axis, forward
        )
        high = lax.ppermute(lax.slice_in_dim(block, 0, width, axis=dim), axis, backward)
        block = jnp.concatenate([low, block, high], axis=dim)
    return block


def gelu_value(values):
    return 0.5 * values * (1.0 + jax.scipy.special.erf(values * root_half))


def gelu_slope(values):
    return (
        0.5 * (1.0 + jax.scipy.special.erf(values * root_half))
        + values * jnp.exp(-0.5 * values * values) * root_two_pi_inv
    )


def depthwise(padded, kernel, rows_out, cols_out, flipped):
    summed = jnp.zeros((rows_out, cols_out, kernel.shape[2]), jnp.float32)
    last_tap = KERNEL - 1
    for row_tap in range(KERNEL):
        for col_tap in range(KERNEL):
            row_start = last_tap - row_tap if flipped else row_tap
            col_start = last_tap - col_tap if flipped else col_tap
            window = padded[row_start : row_start + rows_out, col_start : col_start + cols_out]
            summed = summed + window.astype(jnp.float32) * kernel[row_tap, col_tap]
    return summed


MOST = 4


def extend(image):
    return extended(image, (("sy", 0), ("sx", 1)), KERNEL // 2)


def swapped(array):
    count = lax.axis_size("tp")
    return lax.ppermute(array, "tp", [(i, count - 1 - i) for i in range(count)])


def over_pixels(vector):
    return lax.psum(vector, ("sy", "sx"))


def conv_tiles(windows, kernel):
    summed = jnp.zeros((windows.shape[0], TILE, TILE, windows.shape[3]), jnp.float32)
    for row_tap in range(KERNEL):
        for col_tap in range(KERNEL):
            window = windows[:, row_tap : row_tap + TILE, col_tap : col_tap + TILE]
            summed = summed + window.astype(jnp.float32) * kernel[row_tap, col_tap]
    return summed


def shards(
    features,
    depth_kernel,
    depth_bias,
    norm_gain,
    norm_bias,
    up_weight,
    up_bias,
    response_gain,
    response_shift,
    down_weight,
    down_bias,
    tissue,
    cotangent,
):
    image_rows, image_cols, local_channels = features.shape
    tiles_y, tiles_x = tissue.shape
    tiles = tiles_y * tiles_x
    channels = up_weight.shape[0]
    hidden_total = up_weight.shape[1] * lax.axis_size("tp")
    tp_index = lax.axis_index("tp")
    first = tp_index == 0
    channel_start = tp_index * local_channels
    other_start = (1 - tp_index) * local_channels
    contract_last = (((1,), (1,)), ((), ()))
    pixels = MOST * TILE * TILE
    down_t = lax.all_gather(down_weight.T, ("sy", "sx"), axis=0, tiled=True)
    flags = tissue.reshape(-1)
    tile_ids = jnp.arange(tiles, dtype=jnp.int32)
    earlier = (tile_ids[None, :] < tile_ids[:, None]).astype(jnp.int32)
    ahead = jnp.sum(earlier * flags[None, :], axis=1)
    slot_of = jnp.where(flags > 0, ahead, jnp.sum(flags) + tile_ids - ahead)
    chosen = [jnp.sum(jnp.where(slot_of == s, tile_ids, 0)) for s in range(MOST)]
    slot_mask = jnp.stack([jnp.sum(jnp.where(slot_of == s, flags, 0)) for s in range(MOST)])
    mask_rows = jnp.repeat(slot_mask, TILE * TILE).astype(jnp.float32)

    def windows_of(image, side):
        return jnp.stack(
            [
                lax.dynamic_slice(
                    image,
                    (t // tiles_x * TILE, t % tiles_x * TILE, 0),
                    (side, side, image.shape[2]),
                )
                for t in chosen
            ]
        )

    def spread_out(rows_array):
        held = rows_array.reshape(MOST, TILE, TILE, rows_array.shape[1])
        held = jnp.concatenate([held, jnp.zeros_like(held[:1])], axis=0)
        slots = jnp.minimum(slot_of, MOST)
        rows = []
        for ty in range(tiles_y):
            row = [
                lax.dynamic_index_in_dim(held, slots[ty * tiles_x + tx], 0, keepdims=False)
                for tx in range(tiles_x)
            ]
            rows.append(jnp.concatenate(row, axis=1))
        return jnp.concatenate(rows, axis=0)

    def both_halves(own):
        other = swapped(own)
        return jnp.where(
            first, jnp.concatenate([own, other], axis=1), jnp.concatenate([other, own], axis=1)
        )

    cot_tiles = windows_of(cotangent, TILE).reshape(pixels, local_channels)
    masked_cot = (cot_tiles.astype(jnp.float32) * mask_rows[:, None]).astype(jnp.bfloat16)
    cot_wide = both_halves(masked_cot)
    convolved = conv_tiles(windows_of(extend(features), TILE + KERNEL - 1), depth_kernel)
    convolved = (convolved + depth_bias).astype(jnp.bfloat16).reshape(pixels, local_channels)
    gathered = both_halves(convolved).astype(jnp.float32)
    centre = jnp.mean(gathered, axis=1, keepdims=True)
    spread = jnp.mean(jnp.square(gathered - centre), axis=1, keepdims=True)
    inv_scale = lax.rsqrt(spread + 1e-06)
    standard = (gathered - centre) * inv_scale
    normed = (standard * norm_gain + norm_bias).astype(jnp.bfloat16)
    preact = jnp.dot(normed, up_weight, preferred_element_type=jnp.float32) + up_bias
    hidden = gelu_value(preact).astype(jnp.bfloat16)
    hidden_wide = hidden.astype(jnp.float32)
    squares = over_pixels(jnp.sum(mask_rows[:, None] * hidden_wide * hidden_wide, axis=0))
    column_norms = jnp.sqrt(squares)
    norms_here = jnp.full((8, 128), jnp.sum(column_norms))
    norm_level = (norms_here + swapped(norms_here))[0, 0] / hidden_total + 1e-06
    norm_ratio = column_norms / norm_level
    back_hidden = jnp.dot(cot_wide, down_t, preferred_element_type=jnp.float32)
    products = over_pixels(jnp.sum(back_hidden * hidden_wide, axis=0))
    response = (response_gain * hidden_wide * norm_ratio + response_shift + hidden_wide).astype(
        jnp.bfloat16
    )
    partial_out = lax.dot_general(
        response, down_t, contract_last, preferred_element_type=jnp.float32
    )
    sent_out = lax.dynamic_slice_in_dim(partial_out, other_start, local_channels, 1)
    kept_out = lax.dynamic_slice_in_dim(partial_out, channel_start, local_channels, 1)
    branch = kept_out + swapped(sent_out.astype(jnp.bfloat16)).astype(jnp.float32)
    ratio_grad = response_gain * products
    dots_here = jnp.full((8, 128), jnp.sum(ratio_grad * column_norms))
    dots = (dots_here + swapped(dots_here))[0, 0]
    norms_grad = ratio_grad / norm_level - dots / (hidden_total * norm_level * norm_level)
    hidden_grad = (
        back_hidden * (response_gain * norm_ratio + 1.0)
        + norms_grad * mask_rows[:, None] * hidden_wide / column_norms
    )
    preact_grad = (hidden_grad * gelu_slope(preact)).astype(jnp.bfloat16)
    grad_terms = lax.dot_general(
        preact_grad, up_weight, contract_last, preferred_element_type=jnp.float32
    )
    scaled_terms = grad_terms * norm_gain
    sums_here = jnp.stack([jnp.sum(scaled_terms, axis=1), jnp.sum(scaled_terms * standard, axis=1)])
    sums = sums_here + swapped(sums_here)
    sent_grad = lax.dynamic_slice_in_dim(scaled_terms, other_start, local_channels, 1)
    kept_grad = lax.dynamic_slice_in_dim(scaled_terms, channel_start, local_channels, 1)
    own_standard = lax.dynamic_slice_in_dim(standard, channel_start, local_channels, 1)
    scaled = kept_grad + swapped(sent_grad.astype(jnp.bfloat16)).astype(jnp.float32)
    convolved_grad = inv_scale * (
        scaled - (sums[0] / channels)[:, None] - own_standard * (sums[1] / channels)[:, None]
    )
    grad_image = spread_out(convolved_grad.astype(jnp.bfloat16))
    feature_grad = (
        cotangent.astype(jnp.float32)
        + depthwise(extend(grad_image), depth_kernel, image_rows, image_cols, True)
    ).astype(jnp.bfloat16)
    addend = spread_out(mask_rows[:, None] * (branch + down_bias))
    block_out = (features.astype(jnp.float32) + addend).astype(jnp.bfloat16)
    return (block_out, feature_grad)


def solution(mesh):
    placed = (
        P("sy", "sx", "tp"),
        P(None, None, "tp"),
        P("tp"),
        P(),
        P(),
        P(None, "tp"),
        P("tp"),
        P("tp"),
        P("tp"),
        P("tp", ("sy", "sx")),
        P("tp"),
        P("sy", "sx"),
        P("sy", "sx", "tp"),
    )
    return jax.shard_map(
        shards,
        mesh=mesh,
        in_specs=placed,
        out_specs=(P("sy", "sx", "tp"), P("sy", "sx", "tp")),
        check_vma=False,
    )
```

profile of v0, /device:TPU:12, one launch (start us, length us, event | category | flops | bytes accessed | tf_op | source)
XLA Modules:
  0.0 235.3 jit_solution(2763965542860036640)
XLA Ops:
  7.2 0.7 all-gather.2.cloned.1.call-update
  7.9 1.0 fusion.105
  8.9 3.6 %collective-permute-start = (bf16[3,16,704]{2,1,0:T(8,128)(2,1)S(1)}, bf16[3,16,704]{2,1,0:T(8,128)(2,1)S(1)}, u32[]{:S(2)}, u32[]{:S(2)}) collective-permute-start(bf16[3,16,704]{2,1,0:T(8,128)(2,1)S(1)} %get-tuple-element.90), channel_id=1, source_target_pairs={{0,8},{8,16},{16,24},{1,9},{9,17},{17,25},{2,10},{10,18},{18,26},{... | collective-permute-start | bytes 202760 | tf_op jit(solution)/shard_map/ppermute | solution.py:17
  12.5 2.4 %collective-permute-start.1 = (bf16[3,16,704]{2,1,0:T(8,128)(2,1)S(1)}, bf16[3,16,704]{2,1,0:T(8,128)(2,1)S(1)}, u32[]{:S(2)}, u32[]{:S(2)}) collective-permute-start(bf16[3,16,704]{2,1,0:T(8,128)(2,1)S(1)} %get-tuple-element.89), channel_id=1, source_target_pairs={{8,0},{16,8},{24,16},{9,1},{17,9},{25,17},{10,2},{18,10},{26,18},{... | collective-permute-start | bytes 202760 | tf_op jit(solution)/shard_map/ppermute | solution.py:20
  14.9 0.8 copy.27
  15.9 1.3 reduce_sum.166
  17.3 0.7 broadcast_compare_fusion.1
  17.9 0.8 select_reduce_fusion.8
  28.8 2.7 %add_convert_fusion.4 = f32[4]{0:T(128)S(1)} fusion(s32[1]{0:T(128)} %bitcast.3, s32[1]{0:T(128)} %bitcast.2, s32[1]{0:T(128)} %bitcast.1, s32[1]{0:T(128)} %bitcast), kind=kLoop, calls=%fused_computation.313 | loop fusion | flops 16 | bytes 32 | tf_op jit(solution)/shard_map/convert_element_type | solution.py:107
  31.8 0.2 slice_reduce_fusion.48
  32.2 0.1 fusion.104
  32.4 1.9 collective-permute-start.2
  34.3 3.6 %collective-permute-start.3 = (bf16[30,3,704]{2,1,0:T(4,128)(2,1)S(1)}, bf16[30,3,704]{2,1,0:T(4,128)(2,1)S(1)}, u32[]{:S(2)}, u32[]{:S(2)}) collective-permute-start(bf16[30,3,704]{2,1,0:T(4,128)(2,1)S(1)} %get-tuple-element.86), channel_id=1, source_target_pairs={{2,0},{4,2},{6,4},{3,1},{5,3},{7,5},{10,8},{12,10},{14,12},{11,9},... | collective-permute-start | bytes 380168 | tf_op jit(solution)/shard_map/ppermute | solution.py:20
  38.0 0.2 slice_reduce_fusion.47
  38.1 1.1 collective-permute-done.2
  39.2 1.8 collective-permute-done.3
  41.0 0.6 pad_maximum_fusion.1
  41.6 0.7 dynamic-slice_bitcast_fusion.3
  42.3 0.3 pad_maximum_fusion
  42.6 0.4 copy-done.4
  43.0 5.8 %add_convert_fusion.2 = bf16[4,8,8,704]{3,2,1,0:T(8,128)(2,1)S(1)} fusion(bf16[4,14,14,704]{3,2,1,0:T(8,128)(2,1)S(1)} %pad_maximum_fusion, f32[704]{0:T(1024)S(1)} %copy-done.4, f32[704]{0:T(1024)S(1)} %get-tuple-element.53, f32[704]{0:T(1024)S(1)} %get-tuple-element.54, f32[704]{0:T(1024)S(1)} %get-tuple-element.7, f32[704]{0:T(1024)S(1)} %get-tuple-element.8, ...), kind=kLoop, calls=%fused_computation.138 | loop fusion | flops 26673152 | bytes 18163200 | tf_op jit(solution)/shard_map/convert_element_type | solution.py:144
  48.8 1.6 collective-permute-start.4
  50.5 0.6 collective-permute-start.7
  51.1 0.6 fusion.95
  51.8 9.1 %collective-permute-done.4 = bf16[256,704]{1,0:T(8,128)(2,1)S(1)} collective-permute-done((bf16[256,704]{1,0:T(8,128)(2,1)S(1)}, bf16[256,704]{1,0:T(8,128)(2,1)S(1)}, u32[]{:S(2)}, u32[]{:S(2)}) %collective-permute-start.4) | collective-permute-done | bytes 360480 | tf_op jit(solution)/shard_map/ppermute | solution.py:57
  60.9 0.6 convert_reduce_fusion
  61.5 0.7 fusion.15
  62.2 7.7 %convolution_add_fusion = f32[256,2816]{1,0:T(8,128)} fusion(bf16[1408,2816]{1,0:T(8,128)(2,1)} %param.18, f32[2816]{0:T(1024)S(1)} %copy-done.6, f32[1408]{0:T(1024)S(1)} %copy-done.8, f32[1408]{0:T(1024)S(1)} %copy-done.9, f32[256]{0:T(256)S(1)} %add_rsqrt_fusion, f32[256]{0:T(256)S(1)} %broadcast_multiply_fusion, bf16[256,704]{1,0:T(8,128)(2,1)S(1)} %bitcast.70, ...), kind=kOutput, calls=%fused_computation.47 | convolution fusion | flops 2036170752 | bytes 11558913 | tf_op jit(solution)/shard_map/dot_general | solution.py:151
  69.9 12.2 %all-gather.2.cloned.1.call-done = bf16[1408,2816]{1,0:T(8,128)(2,1)} async-done(((bf16[88,2816]{1,0:T(8,128)(2,1)}), bf16[1408,2816]{1,0:T(8,128)(2,1)}) %all-gather.2.cloned.1.call-update) | async-done | bytes 7929872 | tf_op jit(solution)/shard_map/all_gather | solution.py:99
  82.0 8.3 %fusion.10 = (f32[2816]{0:T(1024)S(1)}, f32[2816]{0:T(1024)S(1)}, bf16[256,2816]{1,0:T(8,128)(2,1)}, f32[256,2816]{1,0:T(8,128)}) fusion(f32[256]{0:T(256)S(1)} %convert_element_type.365, f32[256,2816]{1,0:T(8,128)} %convolution_add_fusion, bf16[1408,2816]{1,0:T(8,128)(2,1)} %all-gather.2.cloned.1.call-done, ...), kind=kOutput, calls=%fused_computation.58 | convolution fusion | flops 2041211392 | bytes 15883265 | tf_op jit(solution)/shard_map/dot_general | solution.py:159
  90.3 48.0 %all-reduce.2 = (f32[2816]{0:T(1024)S(1)}, f32[2816]{0:T(1024)S(1)}) all-reduce(f32[2816]{0:T(1024)S(1)} %get-tuple-element.4, f32[2816]{0:T(1024)S(1)} %get-tuple-element.5), channel_id=1, replica_groups=mesh['sy'=4,'sx'=4,'tp'=2] {'sy','sx'}, use_global_device_ids=true, to_apply=%region_16.17 | all-reduce | flops 5632 | bytes 45056 | tf_op jit(solution)/shard_map/psum | solution.py:61
  138.3 0.7 multiply_reduce_fusion.1
  139.0 0.6 broadcast_in_dim.16
  139.7 1.4 collective-permute-start.5
  141.1 0.7 fusion.106
  153.5 0.7 broadcast_in_dim.17
  154.2 0.7 collective-permute-start.8
  154.9 0.6 broadcast_add_fusion.1
  155.5 0.5 slice.697
  156.7 1.1 collective-permute-done.8
  157.8 0.7 broadcast_add_fusion
  158.5 0.5 slice.704
  159.8 6.3 %fusion.16 = f32[256,1408]{1,0:T(8,128)S(1)} fusion(bf16[1408,2816]{1,0:T(8,128)(2,1)} %all-gather.2.cloned.1.call-done, bf16[256,2816]{1,0:T(8,128)(2,1)} %get-tuple-element.69, f32[2816]{0:T(1024)S(1)} %copy-done.7, f32[2816]{0:T(1024)S(1)} %get-tuple-element.68, f32[2816]{0:T(1024)S(1)} %copy-done.3), kind=kOutput, calls=%fused_computation.109 | convolution fusion | flops 2034368512 | bytes 10847232 | tf_op jit(solution)/shard_map/dot_general | solution.py:164
  166.1 0.2 dynamic-slice_convert_fusion.1
  166.2 0.7 collective-permute-start.6
  167.0 6.9 %fusion.102 = (f32[256]{0:T(256)S(1)}, f32[256]{0:T(256)S(1)}, f32[256,1408]{1,0:T(8,128)S(1)}, f32[256,1408]{1,0:T(8,128)S(1)}) fusion(f32[256]{0:T(256)S(1)} %add_rsqrt_fusion, f32[256]{0:T(256)S(1)} %broadcast_multiply_fusion, bf16[256,704]{1,0:T(8,128)(2,1)S(1)} %bitcast.71, bf16[256,704]{1,0:T(8,128)(2,1)S(1)} %collective-permute-done.4, ...), kind=kOutput, calls=%fused_computation.322 | convolution fusion | flops 2047344128 | bytes 18787840 | tf_op jit(solution)/shard_map/dot_general | solution.py:179
  173.9 1.4 collective-permute-start.10
  175.4 0.2 dynamic-slice_convert_fusion
  175.5 0.7 collective-permute-start.9
  176.2 1.4 collective-permute-done.10
  177.7 5.7 %collective-permute-done.9 = bf16[256,704]{1,0:T(8,128)(2,1)S(1)} collective-permute-done((bf16[256,704]{1,0:T(8,128)(2,1)S(1)}, bf16[256,704]{1,0:T(8,128)(2,1)S(1)}, u32[]{:S(2)}, u32[]{:S(2)}) %collective-permute-start.9) | collective-permute-done | bytes 360480 | tf_op jit(solution)/shard_map/ppermute | solution.py:57
  183.4 0.9 multiply_convert_fusion.1
  184.3 0.1 fusion.91
  184.5 10.4 %collective-permute-start.12 = (bf16[3,16,704]{2,1,0:T(8,128)(2,1)S(1)}, bf16[3,16,704]{2,1,0:T(8,128)(2,1)S(1)}, u32[]{:S(2)}, u32[]{:S(2)}) collective-permute-start(bf16[3,16,704]{2,1,0:T(8,128)(2,1)S(1)} %fusion.93), channel_id=1, source_target_pairs={{8,0},{16,8},{24,16},{9,1},{17,9},{25,17},{10,2},{18,10},{26,18},{... | collective-permute-start | bytes 202760 | tf_op jit(solution)/shard_map/ppermute | solution.py:20
  194.9 1.9 collective-permute-start.11
  196.8 0.2 fusion.81
  197.0 1.0 fusion.28
  197.9 3.2 %collective-permute-done.11 = bf16[3,16,704]{2,1,0:T(8,128)(2,1)S(1)} collective-permute-done((bf16[3,16,704]{2,1,0:T(8,128)(2,1)S(1)}, bf16[3,16,704]{2,1,0:T(8,128)(2,1)S(1)}, u32[]{:S(2)}, u32[]{:S(2)}) %collective-permute-start.11) | collective-permute-done | bytes 67616 | tf_op jit(solution)/shard_map/ppermute | solution.py:17
  201.2 0.1 fusion.103
  201.4 1.9 collective-permute-start.13
  203.3 2.4 %collective-permute-start.14 = (bf16[30,3,704]{2,1,0:T(4,128)(2,1)S(1)}, bf16[30,3,704]{2,1,0:T(4,128)(2,1)S(1)}, u32[]{:S(2)}, u32[]{:S(2)}) collective-permute-start(bf16[30,3,704]{2,1,0:T(4,128)(2,1)S(1)} %get-tuple-element.84), channel_id=1, source_target_pairs={{0,2},{2,4},{4,6},{1,3},{3,5},{5,7},{8,10},{10,12},{12,14},{9,11},... | collective-permute-start | bytes 380168 | tf_op jit(solution)/shard_map/ppermute | solution.py:17
  205.9 0.5 collective-permute-done.13
  206.4 7.1 %collective-permute-done.14 = bf16[30,3,704]{2,1,0:T(4,128)(2,1)S(1)} collective-permute-done((bf16[30,3,704]{2,1,0:T(4,128)(2,1)S(1)}, bf16[30,3,704]{2,1,0:T(4,128)(2,1)S(1)}, u32[]{:S(2)}, u32[]{:S(2)}) %collective-permute-start.14) | collective-permute-done | bytes 126752 | tf_op jit(solution)/shard_map/ppermute | solution.py:17
  213.5 14.9 %add_convert_fusion.1 = bf16[24,16,704]{2,1,0:T(8,128)(2,1)} fusion(bf16[24,16,704]{2,1,0:T(8,128)(2,1)S(1)} %copy-done.1, bf16[30,16,704]{2,1,0:T(8,128)(2,1)S(1)} %constant_dynamic-update-slice_fusion.3, bf16[30,3,704]{2,1,0:T(4,128)(2,1)S(1)} %collective-permute-done.14, bf16[30,3,704]{2,1,0:T(4,128)(2,1)S(1)} %collective-permute-done.13, ...), kind=kLoop, calls=%fused_computation.130 | loop fusion | flops 77316096 | bytes 5933312 | tf_op jit(solution)/shard_map/convert_element_type | solution.py:196
  (59 shorter events, 1.2 us)
Async XLA Ops:
  7.2 24.6 %copy-start.1 = (bf16[24,16,704]{2,1,0:T(8,128)(2,1)S(1)}, bf16[24,16,704]{2,1,0:T(8,128)(2,1)}, u32[]{:S(2)}) copy-start(bf16[24,16,704]{2,1,0:T(8,128)(2,1)} %param.25) | copy-start | bytes 1622020
  7.2 74.8 %all-gather.2.cloned.1.call-start = ((), (), s32[]{:S(2)}) async-start(), calls=%async_computation | async-start | bytes 8425472 | tf_op jit(solution)/shard_map/all_gather | solution.py:99
  7.9 23.9 %copy-start.2 = (f32[7,7,704]{2,1,0:T(8,128)S(1)}, f32[7,7,704]{2,1,0:T(8,128)}, u32[]{:S(2)}) copy-start(f32[7,7,704]{2,1,0:T(8,128)} %param.14) | copy-start | bytes 413956
  8.9 23.2 %copy-start = (bf16[24,16,704]{2,1,0:T(8,128)(2,1)S(1)}, bf16[24,16,704]{2,1,0:T(8,128)(2,1)}, u32[]{:S(2)}) copy-start(bf16[24,16,704]{2,1,0:T(8,128)(2,1)} %param.13) | copy-start | bytes 1622020
  8.9 23.2 %collective-permute-start = (bf16[3,16,704]{2,1,0:T(8,128)(2,1)S(1)}, bf16[3,16,704]{2,1,0:T(8,128)(2,1)S(1)}, u32[]{:S(2)}, u32[]{:S(2)}) collective-permute-start(bf16[3,16,704]{2,1,0:T(8,128)(2,1)S(1)} %get-tuple-element.90), channel_id=1, source_target_pairs={{0,8},{8,16},{16,24},{1,9},{9,17},{17,25},{2,10},{10,18},{18,26},{... | collective-permute-start | bytes 202760 | tf_op jit(solution)/shard_map/ppermute | solution.py:17
  12.5 19.7 %collective-permute-start.1 = (bf16[3,16,704]{2,1,0:T(8,128)(2,1)S(1)}, bf16[3,16,704]{2,1,0:T(8,128)(2,1)S(1)}, u32[]{:S(2)}, u32[]{:S(2)}) collective-permute-start(bf16[3,16,704]{2,1,0:T(8,128)(2,1)S(1)} %get-tuple-element.89), channel_id=1, source_target_pairs={{8,0},{16,8},{24,16},{9,1},{17,9},{25,17},{10,2},{18,10},{26,18},{... | collective-permute-start | bytes 202760 | tf_op jit(solution)/shard_map/ppermute | solution.py:20
  32.4 6.9 %collective-permute-start.2 = (bf16[30,3,704]{2,1,0:T(4,128)(2,1)S(1)}, bf16[30,3,704]{2,1,0:T(4,128)(2,1)S(1)}, u32[]{:S(2)}, u32[]{:S(2)}) collective-permute-start(bf16[30,3,704]{2,1,0:T(4,128)(2,1)S(1)} %get-tuple-element.85), channel_id=1, source_target_pairs={{0,2},{2,4},{4,6},{1,3},{3,5},{5,7},{8,10},{10,12},{12,14},{9,11},... | collective-permute-start | bytes 380168 | tf_op jit(solution)/shard_map/ppermute | solution.py:17
  34.3 6.7 %collective-permute-start.3 = (bf16[30,3,704]{2,1,0:T(4,128)(2,1)S(1)}, bf16[30,3,704]{2,1,0:T(4,128)(2,1)S(1)}, u32[]{:S(2)}, u32[]{:S(2)}) collective-permute-start(bf16[30,3,704]{2,1,0:T(4,128)(2,1)S(1)} %get-tuple-element.86), channel_id=1, source_target_pairs={{2,0},{4,2},{6,4},{3,1},{5,3},{7,5},{10,8},{12,10},{14,12},{11,9},... | collective-permute-start | bytes 380168 | tf_op jit(solution)/shard_map/ppermute | solution.py:20
  42.3 0.7 copy-start.4
  48.8 13.4 %copy-start.6 = (f32[2816]{0:T(1024)S(1)}, f32[2816]{0:T(1024)}, u32[]{:S(2)}) copy-start(f32[2816]{0:T(1024)} %param.19) | copy-start | bytes 33796
  48.8 13.4 %copy-start.8 = (f32[1408]{0:T(1024)S(1)}, f32[1408]{0:T(1024)}, u32[]{:S(2)}) copy-start(f32[1408]{0:T(1024)} %param.17) | copy-start | bytes 16900
  48.8 13.4 %copy-start.9 = (f32[1408]{0:T(1024)S(1)}, f32[1408]{0:T(1024)}, u32[]{:S(2)}) copy-start(f32[1408]{0:T(1024)} %param.16) | copy-start | bytes 16900
  48.8 12.1 %collective-permute-start.4 = (bf16[256,704]{1,0:T(8,128)(2,1)S(1)}, bf16[256,704]{1,0:T(8,128)(2,1)S(1)}, u32[]{:S(2)}, u32[]{:S(2)}) collective-permute-start(bf16[256,704]{1,0:T(8,128)(2,1)S(1)} %bitcast.67), channel_id=1, source_target_pairs={{0,1},{1,0},{2,3},{3,2},{4,5},{5,4},{6,7},{7,6},{8,9},{9,8},{10,11... | collective-permute-start | bytes 1081352 | tf_op jit(solution)/shard_map/ppermute | solution.py:57
  50.5 19.3 %collective-permute-start.7 = (bf16[256,704]{1,0:T(8,128)(2,1)S(1)}, bf16[256,704]{1,0:T(8,128)(2,1)S(1)}, u32[]{:S(2)}, u32[]{:S(2)}) collective-permute-start(bf16[256,704]{1,0:T(8,128)(2,1)S(1)} %fusion.29), channel_id=1, source_target_pairs={{0,1},{1,0},{2,3},{3,2},{4,5},{5,4},{6,7},{7,6},{8,9},{9,8},{10,11... | collective-permute-start | bytes 1081352 | tf_op jit(solution)/shard_map/ppermute | solution.py:57
  69.9 68.5 %copy-start.3 = (f32[2816]{0:T(1024)S(1)}, f32[2816]{0:T(1024)}, u32[]{:S(2)}) copy-start(f32[2816]{0:T(1024)} %param.20) | copy-start | bytes 33796
  69.9 89.9 %copy-start.7 = (f32[2816]{0:T(1024)S(1)}, f32[2816]{0:T(1024)}, u32[]{:S(2)}) copy-start(f32[2816]{0:T(1024)} %param.21) | copy-start | bytes 33796
  139.7 15.2 %collective-permute-start.5 = (f32[8,128]{1,0:T(8,128)S(1)}, f32[8,128]{1,0:T(8,128)S(1)}, u32[]{:S(2)}, u32[]{:S(2)}) collective-permute-start(f32[8,128]{1,0:T(8,128)S(1)} %broadcast_in_dim.16), channel_id=1, source_target_pairs={{0,1},{1,0},{2,3},{3,2},{4,5},{5,4},{6,7},{7,6},{8,9},{9,8},{10,11... | collective-permute-start | bytes 12296 | tf_op jit(solution)/shard_map/ppermute | solution.py:57
  154.2 3.7 %collective-permute-start.8 = (f32[8,128]{1,0:T(8,128)S(1)}, f32[8,128]{1,0:T(8,128)S(1)}, u32[]{:S(2)}, u32[]{:S(2)}) collective-permute-start(f32[8,128]{1,0:T(8,128)S(1)} %broadcast_in_dim.17), channel_id=1, source_target_pairs={{0,1},{1,0},{2,3},{3,2},{4,5},{5,4},{6,7},{7,6},{8,9},{9,8},{10,11... | collective-permute-start | bytes 12296 | tf_op jit(solution)/shard_map/ppermute | solution.py:57
  159.7 7.2 %copy-start.10 = (f32[256,2816]{1,0:T(8,128)S(1)}, f32[256,2816]{1,0:T(8,128)}, u32[]{:S(2)}) copy-start(f32[256,2816]{1,0:T(8,128)} %convolution_add_fusion) | copy-start | bytes 8650756
  159.8 7.2 %copy-start.11 = (f32[256,2816]{1,0:T(8,128)S(1)}, f32[256,2816]{1,0:T(8,128)}, u32[]{:S(2)}) copy-start(f32[256,2816]{1,0:T(8,128)} %get-tuple-element.114) | copy-start | bytes 8650756
  159.8 7.2 %copy-start.12 = (bf16[256,2816]{1,0:T(8,128)(2,1)S(1)}, bf16[256,2816]{1,0:T(8,128)(2,1)}, u32[]{:S(2)}) copy-start(bf16[256,2816]{1,0:T(8,128)(2,1)} %get-tuple-element.69) | copy-start | bytes 4325380
  166.2 11.4 %collective-permute-start.6 = (bf16[256,704]{1,0:T(8,128)(2,1)S(1)}, bf16[256,704]{1,0:T(8,128)(2,1)S(1)}, u32[]{:S(2)}, u32[]{:S(2)}) collective-permute-start(bf16[256,704]{1,0:T(8,128)(2,1)S(1)} %dynamic-slice_convert_fusion.1), channel_id=1, source_target_pairs={{0,1},{1,0},{2,3},{3,2},{4,5},{5,4},{6,7},{7,6},{8,9},{9,8},{10,11... | collective-permute-start | bytes 1081352 | tf_op jit(solution)/shard_map/ppermute | solution.py:57
  167.0 16.4 %copy-start.5 = (f32[704]{0:T(1024)S(1)}, f32[704]{0:T(1024)}, u32[]{:S(2)}) copy-start(f32[704]{0:T(1024)} %param.23) | copy-start | bytes 8452
  173.9 3.7 %collective-permute-start.10 = (f32[2,256]{1,0:T(2,128)S(1)}, f32[2,256]{1,0:T(2,128)S(1)}, u32[]{:S(2)}, u32[]{:S(2)}) collective-permute-start(f32[2,256]{1,0:T(2,128)S(1)} %pad_maximum_fusion.8), channel_id=1, source_target_pairs={{0,1},{1,0},{2,3},{3,2},{4,5},{5,4},{6,7},{7,6},{8,9},{9,8},{10,11... | collective-permute-start | bytes 6152 | tf_op jit(solution)/shard_map/ppermute | solution.py:57
  175.5 7.8 %collective-permute-start.9 = (bf16[256,704]{1,0:T(8,128)(2,1)S(1)}, bf16[256,704]{1,0:T(8,128)(2,1)S(1)}, u32[]{:S(2)}, u32[]{:S(2)}) collective-permute-start(bf16[256,704]{1,0:T(8,128)(2,1)S(1)} %dynamic-slice_convert_fusion), channel_id=1, source_target_pairs={{0,1},{1,0},{2,3},{3,2},{4,5},{5,4},{6,7},{7,6},{8,9},{9,8},{10,11... | collective-permute-start | bytes 1081352 | tf_op jit(solution)/shard_map/ppermute | solution.py:57
  184.5 16.8 %collective-permute-start.12 = (bf16[3,16,704]{2,1,0:T(8,128)(2,1)S(1)}, bf16[3,16,704]{2,1,0:T(8,128)(2,1)S(1)}, u32[]{:S(2)}, u32[]{:S(2)}) collective-permute-start(bf16[3,16,704]{2,1,0:T(8,128)(2,1)S(1)} %fusion.93), channel_id=1, source_target_pairs={{8,0},{16,8},{24,16},{9,1},{17,9},{25,17},{10,2},{18,10},{26,18},{... | collective-permute-start | bytes 202760 | tf_op jit(solution)/shard_map/ppermute | solution.py:20
  194.9 6.2 %collective-permute-start.11 = (bf16[3,16,704]{2,1,0:T(8,128)(2,1)S(1)}, bf16[3,16,704]{2,1,0:T(8,128)(2,1)S(1)}, u32[]{:S(2)}, u32[]{:S(2)}) collective-permute-start(bf16[3,16,704]{2,1,0:T(8,128)(2,1)S(1)} %fusion.94), channel_id=1, source_target_pairs={{0,8},{8,16},{16,24},{1,9},{9,17},{17,25},{2,10},{10,18},{18,26},{... | collective-permute-start | bytes 202760 | tf_op jit(solution)/shard_map/ppermute | solution.py:17
  201.4 5.0 %collective-permute-start.13 = (bf16[30,3,704]{2,1,0:T(4,128)(2,1)S(1)}, bf16[30,3,704]{2,1,0:T(4,128)(2,1)S(1)}, u32[]{:S(2)}, u32[]{:S(2)}) collective-permute-start(bf16[30,3,704]{2,1,0:T(4,128)(2,1)S(1)} %get-tuple-element.83), channel_id=1, source_target_pairs={{2,0},{4,2},{6,4},{3,1},{5,3},{7,5},{10,8},{12,10},{14,12},{11,9},... | collective-permute-start | bytes 380168 | tf_op jit(solution)/shard_map/ppermute | solution.py:20
  203.3 10.2 %collective-permute-start.14 = (bf16[30,3,704]{2,1,0:T(4,128)(2,1)S(1)}, bf16[30,3,704]{2,1,0:T(4,128)(2,1)S(1)}, u32[]{:S(2)}, u32[]{:S(2)}) collective-permute-start(bf16[30,3,704]{2,1,0:T(4,128)(2,1)S(1)} %get-tuple-element.84), channel_id=1, source_target_pairs={{0,2},{2,4},{4,6},{1,3},{3,5},{5,7},{8,10},{10,12},{12,14},{9,11},... | collective-permute-start | bytes 380168 | tf_op jit(solution)/shard_map/ppermute | solution.py:17
Sparse Core Ops, SparseCore 0:
  10.2 71.7 all-gather.1
where the time goes:
time: 236 us; the launch traced here: 235 us
  blocking collectives  48 us (20%)
  waiting for transfers between devices  43.9 us (19%)
  between operations  37.6 us (16%)
  starting transfers between devices  35.4 us (15%)
  other arithmetic  33.5 us (14%)
  matrix products  29.1 us (12%)
  local copies, waits for them, and re-layouts  7.66 us (3%)
    psum x1, blocking collectives, over_pixels(): return lax.psum(vector, ('sy', 'sx'))  48 us
    ppermute x4, starting transfers between devices, extended(): lax.ppermute(lax.slice_in_dim(block, 0, width, axis=dim), axis, backward)  18.3 us
    ppermute x7, waiting for transfers between devices, swapped(): return lax.ppermute(array, 'tp', [(i, count - 1 - i) for i in range(count)])  17.4 us
    convert_element_type x1, other arithmetic, shards(): feature_grad = (cotangent.astype(jnp.float32) + depthwise(extend(grad_ima...  14.9 us
    all_gather x1, waiting for transfers between devices, shards(): down_t = lax.all_gather(down_weight.T, ('sy', 'sx'), axis=0, tiled=True)  12.2 us
    ppermute x4, waiting for transfers between devices, extended(): lax.ppermute(lax.slice_in_dim(block, block.shape[dim] - width, None, axis...  11.4 us
    ppermute x4, starting transfers between devices, extended(): lax.ppermute(lax.slice_in_dim(block, block.shape[dim] - width, None, axis...  9.87 us
    dot_general x1, matrix products, shards(): back_hidden = jnp.dot(cot_wide, down_t, preferred_element_type=jnp.float32)  8.27 us
  transfers between devices with their start and end apart: 16, of which 10 were waited for; matrix products, arithmetic and copies ran while one was open for 15% of the time, Pallas kernels for 0%

commit v1 on v0

--- a/solution.py
+++ b/solution.py
@@ -1,3 +1,4 @@
+import functools
 import jax
 import jax.numpy as jnp
 from jax import lax
@@ -7,6 +8,15 @@
 TILE = 8
 root_half = 0.7071067811865476
 root_two_pi_inv = 0.3989422804014327
+
+
+def reach_masks(z, group_axis, along_axis):
+    for nth in (group_axis, along_axis):
+        z = lax.psum(z, nth)
+    return z
+
+
+load_sites = functools.partial(reach_masks, group_axis="sx", along_axis="sy")
 
 
 def extended(block, sides, width):
@@ -58,7 +68,7 @@
 
 
 def over_pixels(vector):
-    return lax.psum(vector, ("sy", "sx"))
+    return load_sites(vector)
 
 
 def conv_tiles(windows, kernel):

time: 236 us -> 206 us (0.87)
  blocking collectives: 48 us -> 26.1 us
  starting transfers between devices: 35.4 us -> 30.3 us
  waiting for transfers between devices: 43.9 us -> 40.8 us
    psum x1 -> x2, blocking collectives: 48 us -> 26.1 us  [reach_masks(): z = lax.psum(z, nth)]
    ppermute x4, starting transfers between devices: 18.3 us -> 13.3 us  [extended(): lax.ppermute(lax.slice_in_dim(block, 0, width, axis=dim), axis, backward)]
    ppermute x4, waiting for transfers between devices: 11.4 us -> 8.13 us  [extended(): lax.ppermute(lax.slice_in_dim(block, block.shape[dim] - width, None, axis...]
  transfers between devices with their start and end apart: 16 -> 16, of which waited for: 10 -> 10; matrix products, arithmetic and copies ran while one was open for 15% -> 18% of each run, Pallas kernels for 0% -> 0%
where the time goes in v1:
time: 206 us; the launch traced here: 205 us
  waiting for transfers between devices  40.8 us (20%)
  between operations  37.6 us (18%)
  other arithmetic  33.4 us (16%)
  starting transfers between devices  30.3 us (15%)
  matrix products  29.1 us (14%)
  blocking collectives  26.1 us (13%)
  local copies, waits for them, and re-layouts  7.67 us (4%)
    psum x2, blocking collectives, reach_masks(): z = lax.psum(z, nth)  26.1 us
    ppermute x7, waiting for transfers between devices, swapped(): return lax.ppermute(array, 'tp', [(i, count - 1 - i) for i in range(count)])  17.5 us
    convert_element_type x1, other arithmetic, shards(): feature_grad = (cotangent.astype(jnp.float32) + depthwise(extend(grad_ima...  14.9 us
    ppermute x4, starting transfers between devices, extended(): lax.ppermute(lax.slice_in_dim(block, 0, width, axis=dim), axis, backward)  13.3 us
    all_gather x1, waiting for transfers between devices, shards(): down_t = lax.all_gather(down_weight.T, ('sy', 'sx'), axis=0, tiled=True)  12.1 us
    ppermute x4, starting transfers between devices, extended(): lax.ppermute(lax.slice_in_dim(block, block.shape[dim] - width, None, axis...  9.87 us
    dot_general x1, matrix products, shards(): back_hidden = jnp.dot(cot_wide, down_t, preferred_element_type=jnp.float32)  8.26 us
    ppermute x4, waiting for transfers between devices, extended(): lax.ppermute(lax.slice_in_dim(block, block.shape[dim] - width, None, axis...  8.13 us
  transfers between devices with their start and end apart: 16, of which 10 were waited for; matrix products, arithmetic and copies ran while one was open for 18% of the time, Pallas kernels for 0%

profile of v1, /device:TPU:12, one launch (start us, length us, event | category | flops | bytes accessed | tf_op | source)
XLA Modules:
  0.0 205.0 jit_solution(6884685768434847341)
XLA Ops:
  7.2 0.7 all-gather.2.cloned.1.call-update
  7.9 1.0 fusion.105
  8.9 3.6 %collective-permute-start = (bf16[3,16,704]{2,1,0:T(8,128)(2,1)S(1)}, bf16[3,16,704]{2,1,0:T(8,128)(2,1)S(1)}, u32[]{:S(2)}, u32[]{:S(2)}) collective-permute-start(bf16[3,16,704]{2,1,0:T(8,128)(2,1)S(1)} %get-tuple-element.92), channel_id=1, source_target_pairs={{0,8},{8,16},{16,24},{1,9},{9,17},{17,25},{2,10},{10,18},{18,26},{... | collective-permute-start | bytes 202760 | tf_op jit(solution)/shard_map/ppermute | solution.py:27
  12.5 2.4 %collective-permute-start.1 = (bf16[3,16,704]{2,1,0:T(8,128)(2,1)S(1)}, bf16[3,16,704]{2,1,0:T(8,128)(2,1)S(1)}, u32[]{:S(2)}, u32[]{:S(2)}) collective-permute-start(bf16[3,16,704]{2,1,0:T(8,128)(2,1)S(1)} %get-tuple-element.91), channel_id=1, source_target_pairs={{8,0},{16,8},{24,16},{9,1},{17,9},{25,17},{10,2},{18,10},{26,18},{... | collective-permute-start | bytes 202760 | tf_op jit(solution)/shard_map/ppermute | solution.py:30
  14.9 0.8 copy.27
  15.9 1.3 reduce_sum.166
  17.3 0.7 broadcast_compare_fusion.1
  17.9 0.8 select_reduce_fusion.8
  28.8 2.7 %add_convert_fusion.4 = f32[4]{0:T(128)S(1)} fusion(s32[1]{0:T(128)} %bitcast.3, s32[1]{0:T(128)} %bitcast.2, s32[1]{0:T(128)} %bitcast.1, s32[1]{0:T(128)} %bitcast), kind=kLoop, calls=%fused_computation.313 | loop fusion | flops 16 | bytes 32 | tf_op jit(solution)/shard_map/convert_element_type | solution.py:117
  31.8 0.2 slice_reduce_fusion.48
  32.2 0.1 fusion.104
  32.4 1.9 collective-permute-start.2
  34.3 3.6 %collective-permute-start.3 = (bf16[30,3,704]{2,1,0:T(4,128)(2,1)S(1)}, bf16[30,3,704]{2,1,0:T(4,128)(2,1)S(1)}, u32[]{:S(2)}, u32[]{:S(2)}) collective-permute-start(bf16[30,3,704]{2,1,0:T(4,128)(2,1)S(1)} %get-tuple-element.88), channel_id=1, source_target_pairs={{2,0},{4,2},{6,4},{3,1},{5,3},{7,5},{10,8},{12,10},{14,12},{11,9},... | collective-permute-start | bytes 380168 | tf_op jit(solution)/shard_map/ppermute | solution.py:30
  38.0 0.2 slice_reduce_fusion.47
  38.1 1.1 collective-permute-done.2
  39.2 1.8 collective-permute-done.3
  41.0 0.6 pad_maximum_fusion.1
  41.6 0.7 dynamic-slice_bitcast_fusion.3
  42.3 0.3 pad_maximum_fusion
  42.6 0.4 copy-done.4
  43.0 5.8 %add_convert_fusion.2 = bf16[4,8,8,704]{3,2,1,0:T(8,128)(2,1)S(1)} fusion(bf16[4,14,14,704]{3,2,1,0:T(8,128)(2,1)S(1)} %pad_maximum_fusion, f32[704]{0:T(1024)S(1)} %copy-done.4, f32[704]{0:T(1024)S(1)} %get-tuple-element.53, f32[704]{0:T(1024)S(1)} %get-tuple-element.54, f32[704]{0:T(1024)S(1)} %get-tuple-element.7, f32[704]{0:T(1024)S(1)} %get-tuple-element.8, ...), kind=kLoop, calls=%fused_computation.138 | loop fusion | flops 26673152 | bytes 18163200 | tf_op jit(solution)/shard_map/convert_element_type | solution.py:154
  48.8 1.6 collective-permute-start.4
  50.5 0.6 collective-permute-start.7
  51.1 0.6 fusion.95
  51.8 9.1 %collective-permute-done.4 = bf16[256,704]{1,0:T(8,128)(2,1)S(1)} collective-permute-done((bf16[256,704]{1,0:T(8,128)(2,1)S(1)}, bf16[256,704]{1,0:T(8,128)(2,1)S(1)}, u32[]{:S(2)}, u32[]{:S(2)}) %collective-permute-start.4) | collective-permute-done | bytes 360480 | tf_op jit(solution)/shard_map/ppermute | solution.py:67
  60.9 0.6 convert_reduce_fusion
  61.5 0.7 fusion.15
  62.2 7.7 %convolution_add_fusion = f32[256,2816]{1,0:T(8,128)} fusion(bf16[1408,2816]{1,0:T(8,128)(2,1)} %param.18, f32[2816]{0:T(1024)S(1)} %copy-done.6, f32[1408]{0:T(1024)S(1)} %copy-done.8, f32[1408]{0:T(1024)S(1)} %copy-done.9, f32[256]{0:T(256)S(1)} %add_rsqrt_fusion, f32[256]{0:T(256)S(1)} %broadcast_multiply_fusion, bf16[256,704]{1,0:T(8,128)(2,1)S(1)} %bitcast.70, ...), kind=kOutput, calls=%fused_computation.47 | convolution fusion | flops 2036170752 | bytes 11558913 | tf_op jit(solution)/shard_map/dot_general | solution.py:161
  69.9 12.1 %all-gather.2.cloned.1.call-done = bf16[1408,2816]{1,0:T(8,128)(2,1)} async-done(((bf16[88,2816]{1,0:T(8,128)(2,1)}), bf16[1408,2816]{1,0:T(8,128)(2,1)}) %all-gather.2.cloned.1.call-update) | async-done | bytes 7929872 | tf_op jit(solution)/shard_map/all_gather | solution.py:109
  82.0 8.3 %fusion.10 = (f32[2816]{0:T(1024)S(1)}, f32[2816]{0:T(1024)S(1)}, bf16[256,2816]{1,0:T(8,128)(2,1)}, f32[256,2816]{1,0:T(8,128)}) fusion(f32[256]{0:T(256)S(1)} %convert_element_type.365, f32[256,2816]{1,0:T(8,128)} %convolution_add_fusion, bf16[1408,2816]{1,0:T(8,128)(2,1)} %all-gather.2.cloned.1.call-done, ...), kind=kOutput, calls=%fused_computation.58 | convolution fusion | flops 2041211392 | bytes 15883265 | tf_op jit(solution)/shard_map/dot_general | solution.py:169
  90.3 11.4 %all-reduce.2 = (f32[2816]{0:T(1024)S(1)}, f32[2816]{0:T(1024)S(1)}) all-reduce(f32[2816]{0:T(1024)S(1)} %get-tuple-element.4, f32[2816]{0:T(1024)S(1)} %get-tuple-element.5), channel_id=1, replica_groups=mesh['sy'=4,'sx'=4,'tp'=2] {'sx'}, use_global_device_ids=true, to_apply=%region_17.18 | all-reduce | flops 5632 | bytes 45056 | tf_op jit(solution)/shard_map/psum | solution.py:15
  101.7 14.7 %all-reduce.3 = (f32[2816]{0:T(1024)S(1)}, f32[2816]{0:T(1024)S(1)}) all-reduce(f32[2816]{0:T(1024)S(1)} %get-tuple-element.65, f32[2816]{0:T(1024)S(1)} %get-tuple-element.66), channel_id=1, replica_groups=mesh['sy'=4,'sx'=4,'tp'=2] {'sy'}, use_global_device_ids=true, to_apply=%region_18.19 | all-reduce | flops 5632 | bytes 45056 | tf_op jit(solution)/shard_map/psum | solution.py:15
  116.4 0.7 multiply_reduce_fusion.1
  117.1 0.6 broadcast_in_dim.16
  117.7 1.5 collective-permute-start.5
  119.3 0.7 fusion.106
  131.6 0.7 broadcast_in_dim.17
  132.3 0.6 collective-permute-start.8
  133.0 0.6 broadcast_add_fusion.1
  133.6 0.5 slice.697
  134.8 1.2 collective-permute-done.8
  136.0 0.7 broadcast_add_fusion
  136.7 0.5 slice.704
  137.9 6.3 %fusion.16 = f32[256,1408]{1,0:T(8,128)S(1)} fusion(bf16[1408,2816]{1,0:T(8,128)(2,1)} %all-gather.2.cloned.1.call-done, bf16[256,2816]{1,0:T(8,128)(2,1)} %get-tuple-element.71, f32[2816]{0:T(1024)S(1)} %copy-done.7, f32[2816]{0:T(1024)S(1)} %get-tuple-element.70, f32[2816]{0:T(1024)S(1)} %copy-done.3), kind=kOutput, calls=%fused_computation.109 | convolution fusion | flops 2034368512 | bytes 10847232 | tf_op jit(solution)/shard_map/dot_general | solution.py:174
  144.2 0.2 dynamic-slice_convert_fusion.1
  144.4 0.6 collective-permute-start.6
  145.0 6.9 %fusion.102 = (f32[256]{0:T(256)S(1)}, f32[256]{0:T(256)S(1)}, f32[256,1408]{1,0:T(8,128)S(1)}, f32[256,1408]{1,0:T(8,128)S(1)}) fusion(f32[256]{0:T(256)S(1)} %add_rsqrt_fusion, f32[256]{0:T(256)S(1)} %broadcast_multiply_fusion, bf16[256,704]{1,0:T(8,128)(2,1)S(1)} %bitcast.71, bf16[256,704]{1,0:T(8,128)(2,1)S(1)} %collective-permute-done.4, ...), kind=kOutput, calls=%fused_computation.322 | convolution fusion | flops 2047344128 | bytes 18787840 | tf_op jit(solution)/shard_map/dot_general | solution.py:189
  151.9 1.5 collective-permute-start.10
  153.4 0.2 dynamic-slice_convert_fusion
  153.6 0.6 collective-permute-start.9
  154.3 1.4 collective-permute-done.10
  155.7 5.8 %collective-permute-done.9 = bf16[256,704]{1,0:T(8,128)(2,1)S(1)} collective-permute-done((bf16[256,704]{1,0:T(8,128)(2,1)S(1)}, bf16[256,704]{1,0:T(8,128)(2,1)S(1)}, u32[]{:S(2)}, u32[]{:S(2)}) %collective-permute-start.9) | collective-permute-done | bytes 360480 | tf_op jit(solution)/shard_map/ppermute | solution.py:67
  161.5 0.9 multiply_convert_fusion.1
  162.5 5.4 %collective-permute-start.12 = (bf16[3,16,704]{2,1,0:T(8,128)(2,1)S(1)}, bf16[3,16,704]{2,1,0:T(8,128)(2,1)S(1)}, u32[]{:S(2)}, u32[]{:S(2)}) collective-permute-start(bf16[3,16,704]{2,1,0:T(8,128)(2,1)S(1)} %fusion.93), channel_id=1, source_target_pairs={{8,0},{16,8},{24,16},{9,1},{17,9},{25,17},{10,2},{18,10},{26,18},{... | collective-permute-start | bytes 202760 | tf_op jit(solution)/shard_map/ppermute | solution.py:30
  168.0 1.9 collective-permute-start.11
  169.9 0.2 fusion.81
  170.1 1.0 fusion.28
  171.0 3.2 %collective-permute-done.11 = bf16[3,16,704]{2,1,0:T(8,128)(2,1)S(1)} collective-permute-done((bf16[3,16,704]{2,1,0:T(8,128)(2,1)S(1)}, bf16[3,16,704]{2,1,0:T(8,128)(2,1)S(1)}, u32[]{:S(2)}, u32[]{:S(2)}) %collective-permute-start.11) | collective-permute-done | bytes 67616 | tf_op jit(solution)/shard_map/ppermute | solution.py:27
  174.3 0.1 fusion.103
  174.5 1.9 collective-permute-start.13
  176.4 2.4 %collective-permute-start.14 = (bf16[30,3,704]{2,1,0:T(4,128)(2,1)S(1)}, bf16[30,3,704]{2,1,0:T(4,128)(2,1)S(1)}, u32[]{:S(2)}, u32[]{:S(2)}) collective-permute-start(bf16[30,3,704]{2,1,0:T(4,128)(2,1)S(1)} %get-tuple-element.86), channel_id=1, source_target_pairs={{0,2},{2,4},{4,6},{1,3},{3,5},{5,7},{8,10},{10,12},{12,14},{9,11},... | collective-permute-start | bytes 380168 | tf_op jit(solution)/shard_map/ppermute | solution.py:27
  178.9 0.5 collective-permute-done.13
  179.5 3.8 %collective-permute-done.14 = bf16[30,3,704]{2,1,0:T(4,128)(2,1)S(1)} collective-permute-done((bf16[30,3,704]{2,1,0:T(4,128)(2,1)S(1)}, bf16[30,3,704]{2,1,0:T(4,128)(2,1)S(1)}, u32[]{:S(2)}, u32[]{:S(2)}) %collective-permute-start.14) | collective-permute-done | bytes 126752 | tf_op jit(solution)/shard_map/ppermute | solution.py:27
  183.3 14.9 %add_convert_fusion.1 = bf16[24,16,704]{2,1,0:T(8,128)(2,1)} fusion(bf16[24,16,704]{2,1,0:T(8,128)(2,1)S(1)} %copy-done.1, bf16[30,16,704]{2,1,0:T(8,128)(2,1)S(1)} %constant_dynamic-update-slice_fusion.3, bf16[30,3,704]{2,1,0:T(4,128)(2,1)S(1)} %collective-permute-done.14, bf16[30,3,704]{2,1,0:T(4,128)(2,1)S(1)} %collective-permute-done.13, ...), kind=kLoop, calls=%fused_computation.130 | loop fusion | flops 77316096 | bytes 5933312 | tf_op jit(solution)/shard_map/convert_element_type | solution.py:206
  (60 shorter events, 1.3 us)
Async XLA Ops:
  7.2 24.6 %copy-start.1 = (bf16[24,16,704]{2,1,0:T(8,128)(2,1)S(1)}, bf16[24,16,704]{2,1,0:T(8,128)(2,1)}, u32[]{:S(2)}) copy-start(bf16[24,16,704]{2,1,0:T(8,128)(2,1)} %param.25) | copy-start | bytes 1622020
  7.2 74.8 %all-gather.2.cloned.1.call-start = ((), (), s32[]{:S(2)}) async-start(), calls=%async_computation | async-start | bytes 8425472 | tf_op jit(solution)/shard_map/all_gather | solution.py:109
  7.9 23.9 %copy-start.2 = (f32[7,7,704]{2,1,0:T(8,128)S(1)}, f32[7,7,704]{2,1,0:T(8,128)}, u32[]{:S(2)}) copy-start(f32[7,7,704]{2,1,0:T(8,128)} %param.14) | copy-start | bytes 413956
  8.9 23.2 %copy-start = (bf16[24,16,704]{2,1,0:T(8,128)(2,1)S(1)}, bf16[24,16,704]{2,1,0:T(8,128)(2,1)}, u32[]{:S(2)}) copy-start(bf16[24,16,704]{2,1,0:T(8,128)(2,1)} %param.13) | copy-start | bytes 1622020
  8.9 23.2 %collective-permute-start = (bf16[3,16,704]{2,1,0:T(8,128)(2,1)S(1)}, bf16[3,16,704]{2,1,0:T(8,128)(2,1)S(1)}, u32[]{:S(2)}, u32[]{:S(2)}) collective-permute-start(bf16[3,16,704]{2,1,0:T(8,128)(2,1)S(1)} %get-tuple-element.92), channel_id=1, source_target_pairs={{0,8},{8,16},{16,24},{1,9},{9,17},{17,25},{2,10},{10,18},{18,26},{... | collective-permute-start | bytes 202760 | tf_op jit(solution)/shard_map/ppermute | solution.py:27
  12.5 19.7 %collective-permute-start.1 = (bf16[3,16,704]{2,1,0:T(8,128)(2,1)S(1)}, bf16[3,16,704]{2,1,0:T(8,128)(2,1)S(1)}, u32[]{:S(2)}, u32[]{:S(2)}) collective-permute-start(bf16[3,16,704]{2,1,0:T(8,128)(2,1)S(1)} %get-tuple-element.91), channel_id=1, source_target_pairs={{8,0},{16,8},{24,16},{9,1},{17,9},{25,17},{10,2},{18,10},{26,18},{... | collective-permute-start | bytes 202760 | tf_op jit(solution)/shard_map/ppermute | solution.py:30
  32.4 6.9 %collective-permute-start.2 = (bf16[30,3,704]{2,1,0:T(4,128)(2,1)S(1)}, bf16[30,3,704]{2,1,0:T(4,128)(2,1)S(1)}, u32[]{:S(2)}, u32[]{:S(2)}) collective-permute-start(bf16[30,3,704]{2,1,0:T(4,128)(2,1)S(1)} %get-tuple-element.87), channel_id=1, source_target_pairs={{0,2},{2,4},{4,6},{1,3},{3,5},{5,7},{8,10},{10,12},{12,14},{9,11},... | collective-permute-start | bytes 380168 | tf_op jit(solution)/shard_map/ppermute | solution.py:27
  34.3 6.7 %collective-permute-start.3 = (bf16[30,3,704]{2,1,0:T(4,128)(2,1)S(1)}, bf16[30,3,704]{2,1,0:T(4,128)(2,1)S(1)}, u32[]{:S(2)}, u32[]{:S(2)}) collective-permute-start(bf16[30,3,704]{2,1,0:T(4,128)(2,1)S(1)} %get-tuple-element.88), channel_id=1, source_target_pairs={{2,0},{4,2},{6,4},{3,1},{5,3},{7,5},{10,8},{12,10},{14,12},{11,9},... | collective-permute-start | bytes 380168 | tf_op jit(solution)/shard_map/ppermute | solution.py:30
  42.3 0.7 copy-start.4
  48.8 13.4 %copy-start.6 = (f32[2816]{0:T(1024)S(1)}, f32[2816]{0:T(1024)}, u32[]{:S(2)}) copy-start(f32[2816]{0:T(1024)} %param.19) | copy-start | bytes 33796
  48.8 13.4 %copy-start.8 = (f32[1408]{0:T(1024)S(1)}, f32[1408]{0:T(1024)}, u32[]{:S(2)}) copy-start(f32[1408]{0:T(1024)} %param.17) | copy-start | bytes 16900
  48.8 13.4 %copy-start.9 = (f32[1408]{0:T(1024)S(1)}, f32[1408]{0:T(1024)}, u32[]{:S(2)}) copy-start(f32[1408]{0:T(1024)} %param.16) | copy-start | bytes 16900
  48.8 12.1 %collective-permute-start.4 = (bf16[256,704]{1,0:T(8,128)(2,1)S(1)}, bf16[256,704]{1,0:T(8,128)(2,1)S(1)}, u32[]{:S(2)}, u32[]{:S(2)}) collective-permute-start(bf16[256,704]{1,0:T(8,128)(2,1)S(1)} %bitcast.67), channel_id=1, source_target_pairs={{0,1},{1,0},{2,3},{3,2},{4,5},{5,4},{6,7},{7,6},{8,9},{9,8},{10,11... | collective-permute-start | bytes 1081352 | tf_op jit(solution)/shard_map/ppermute | solution.py:67
  50.5 19.3 %collective-permute-start.7 = (bf16[256,704]{1,0:T(8,128)(2,1)S(1)}, bf16[256,704]{1,0:T(8,128)(2,1)S(1)}, u32[]{:S(2)}, u32[]{:S(2)}) collective-permute-start(bf16[256,704]{1,0:T(8,128)(2,1)S(1)} %fusion.29), channel_id=1, source_target_pairs={{0,1},{1,0},{2,3},{3,2},{4,5},{5,4},{6,7},{7,6},{8,9},{9,8},{10,11... | collective-permute-start | bytes 1081352 | tf_op jit(solution)/shard_map/ppermute | solution.py:67
  69.9 46.5 %copy-start.3 = (f32[2816]{0:T(1024)S(1)}, f32[2816]{0:T(1024)}, u32[]{:S(2)}) copy-start(f32[2816]{0:T(1024)} %param.20) | copy-start | bytes 33796
  69.9 68.0 %copy-start.7 = (f32[2816]{0:T(1024)S(1)}, f32[2816]{0:T(1024)}, u32[]{:S(2)}) copy-start(f32[2816]{0:T(1024)} %param.21) | copy-start | bytes 33796
  117.7 15.2 %collective-permute-start.5 = (f32[8,128]{1,0:T(8,128)S(1)}, f32[8,128]{1,0:T(8,128)S(1)}, u32[]{:S(2)}, u32[]{:S(2)}) collective-permute-start(f32[8,128]{1,0:T(8,128)S(1)} %broadcast_in_dim.16), channel_id=1, source_target_pairs={{0,1},{1,0},{2,3},{3,2},{4,5},{5,4},{6,7},{7,6},{8,9},{9,8},{10,11... | collective-permute-start | bytes 12296 | tf_op jit(solution)/shard_map/ppermute | solution.py:67
  132.3 3.7 %collective-permute-start.8 = (f32[8,128]{1,0:T(8,128)S(1)}, f32[8,128]{1,0:T(8,128)S(1)}, u32[]{:S(2)}, u32[]{:S(2)}) collective-permute-start(f32[8,128]{1,0:T(8,128)S(1)} %broadcast_in_dim.17), channel_id=1, source_target_pairs={{0,1},{1,0},{2,3},{3,2},{4,5},{5,4},{6,7},{7,6},{8,9},{9,8},{10,11... | collective-permute-start | bytes 12296 | tf_op jit(solution)/shard_map/ppermute | solution.py:67
  137.9 7.1 %copy-start.10 = (f32[256,2816]{1,0:T(8,128)S(1)}, f32[256,2816]{1,0:T(8,128)}, u32[]{:S(2)}) copy-start(f32[256,2816]{1,0:T(8,128)} %convolution_add_fusion) | copy-start | bytes 8650756
  137.9 7.1 %copy-start.11 = (f32[256,2816]{1,0:T(8,128)S(1)}, f32[256,2816]{1,0:T(8,128)}, u32[]{:S(2)}) copy-start(f32[256,2816]{1,0:T(8,128)} %get-tuple-element.116) | copy-start | bytes 8650756
  137.9 7.1 %copy-start.12 = (bf16[256,2816]{1,0:T(8,128)(2,1)S(1)}, bf16[256,2816]{1,0:T(8,128)(2,1)}, u32[]{:S(2)}) copy-start(bf16[256,2816]{1,0:T(8,128)(2,1)} %get-tuple-element.71) | copy-start | bytes 4325380
  144.4 11.3 %collective-permute-start.6 = (bf16[256,704]{1,0:T(8,128)(2,1)S(1)}, bf16[256,704]{1,0:T(8,128)(2,1)S(1)}, u32[]{:S(2)}, u32[]{:S(2)}) collective-permute-start(bf16[256,704]{1,0:T(8,128)(2,1)S(1)} %dynamic-slice_convert_fusion.1), channel_id=1, source_target_pairs={{0,1},{1,0},{2,3},{3,2},{4,5},{5,4},{6,7},{7,6},{8,9},{9,8},{10,11... | collective-permute-start | bytes 1081352 | tf_op jit(solution)/shard_map/ppermute | solution.py:67
  145.0 16.4 %copy-start.5 = (f32[704]{0:T(1024)S(1)}, f32[704]{0:T(1024)}, u32[]{:S(2)}) copy-start(f32[704]{0:T(1024)} %param.23) | copy-start | bytes 8452
  151.9 3.7 %collective-permute-start.10 = (f32[2,256]{1,0:T(2,128)S(1)}, f32[2,256]{1,0:T(2,128)S(1)}, u32[]{:S(2)}, u32[]{:S(2)}) collective-permute-start(f32[2,256]{1,0:T(2,128)S(1)} %pad_maximum_fusion.8), channel_id=1, source_target_pairs={{0,1},{1,0},{2,3},{3,2},{4,5},{5,4},{6,7},{7,6},{8,9},{9,8},{10,11... | collective-permute-start | bytes 6152 | tf_op jit(solution)/shard_map/ppermute | solution.py:67
  153.6 7.8 %collective-permute-start.9 = (bf16[256,704]{1,0:T(8,128)(2,1)S(1)}, bf16[256,704]{1,0:T(8,128)(2,1)S(1)}, u32[]{:S(2)}, u32[]{:S(2)}) collective-permute-start(bf16[256,704]{1,0:T(8,128)(2,1)S(1)} %dynamic-slice_convert_fusion), channel_id=1, source_target_pairs={{0,1},{1,0},{2,3},{3,2},{4,5},{5,4},{6,7},{7,6},{8,9},{9,8},{10,11... | collective-permute-start | bytes 1081352 | tf_op jit(solution)/shard_map/ppermute | solution.py:67
  162.5 11.8 %collective-permute-start.12 = (bf16[3,16,704]{2,1,0:T(8,128)(2,1)S(1)}, bf16[3,16,704]{2,1,0:T(8,128)(2,1)S(1)}, u32[]{:S(2)}, u32[]{:S(2)}) collective-permute-start(bf16[3,16,704]{2,1,0:T(8,128)(2,1)S(1)} %fusion.93), channel_id=1, source_target_pairs={{8,0},{16,8},{24,16},{9,1},{17,9},{25,17},{10,2},{18,10},{26,18},{... | collective-permute-start | bytes 202760 | tf_op jit(solution)/shard_map/ppermute | solution.py:30
  168.0 6.2 %collective-permute-start.11 = (bf16[3,16,704]{2,1,0:T(8,128)(2,1)S(1)}, bf16[3,16,704]{2,1,0:T(8,128)(2,1)S(1)}, u32[]{:S(2)}, u32[]{:S(2)}) collective-permute-start(bf16[3,16,704]{2,1,0:T(8,128)(2,1)S(1)} %fusion.94), channel_id=1, source_target_pairs={{0,8},{8,16},{16,24},{1,9},{9,17},{17,25},{2,10},{10,18},{18,26},{... | collective-permute-start | bytes 202760 | tf_op jit(solution)/shard_map/ppermute | solution.py:27
  174.5 5.0 %collective-permute-start.13 = (bf16[30,3,704]{2,1,0:T(4,128)(2,1)S(1)}, bf16[30,3,704]{2,1,0:T(4,128)(2,1)S(1)}, u32[]{:S(2)}, u32[]{:S(2)}) collective-permute-start(bf16[30,3,704]{2,1,0:T(4,128)(2,1)S(1)} %get-tuple-element.85), channel_id=1, source_target_pairs={{2,0},{4,2},{6,4},{3,1},{5,3},{7,5},{10,8},{12,10},{14,12},{11,9},... | collective-permute-start | bytes 380168 | tf_op jit(solution)/shard_map/ppermute | solution.py:30
  176.4 6.9 %collective-permute-start.14 = (bf16[30,3,704]{2,1,0:T(4,128)(2,1)S(1)}, bf16[30,3,704]{2,1,0:T(4,128)(2,1)S(1)}, u32[]{:S(2)}, u32[]{:S(2)}) collective-permute-start(bf16[30,3,704]{2,1,0:T(4,128)(2,1)S(1)} %get-tuple-element.86), channel_id=1, source_target_pairs={{0,2},{2,4},{4,6},{1,3},{3,5},{5,7},{8,10},{10,12},{12,14},{9,11},... | collective-permute-start | bytes 380168 | tf_op jit(solution)/shard_map/ppermute | solution.py:27
Sparse Core Ops, SparseCore 0:
  10.2 71.7 all-gather.1
